TPU v7x, 256 devices: a whole 4x4x8 slice. The times are simulated.
256 devices in a mesh: lat: 32 (over z, y_hi, core), ma: 8 (over x, y_lo).
Axes of the slice: x: 4, y: 4 (y_hi: 2, y_lo: 2; y = y_hi * 2 + y_lo), z: 8, core: 2. Of those that a mesh axis runs over, the one named last changes fastest.
Arguments:
- spectral: bfloat16 [64, 2, 648, 768], P('ma'), may hold values from -0.25 to 0.25
- set_pair: int32 [64], P('ma'), may hold values from 0 to 639, as said below
- lat_sines: float32 [1280], replicated, may hold values from 0.005 to 0.3
Outputs:
- grid: bfloat16 [2560, 64, 2, 768], P(('lat', 'ma'))
Inputs may be any that keep to these rules, and one draw needn't show every extreme that they name: `set_pair`: the values are distinct; 0 and 639 both occur.
All inputs are finite; a program needn't handle non-finite values.
Results may differ from a plain program's by a relative error of at most 0.0058.
Values may be sent and summed in bfloat16 or wider, within the bound.
A program may use at most 128 MiB of HBM per device.

v0:
```python
import jax
import jax.numpy as jnp
from jax import lax
from jax.sharding import PartitionSpec as P

M = 1280
NH = 648
BAND = 80


def legendre_runs(sines, pairs):
    span_size = 128
    block_count = (M + 1 + span_size - 1) // span_size
    padded_length = block_count * span_size
    set_count = pairs.shape[0]
    positions = jnp.arange(padded_length, dtype=jnp.int32)[None, :]
    run_length = (M - pairs)[:, None]
    first_run = positions < run_length
    inside = positions <= M
    order_m = jnp.where(first_run, pairs[:, None], M - 1 - pairs[:, None]).astype(jnp.float32)
    offset_k = jnp.where(first_run, positions, positions - run_length).astype(jnp.float32)
    degree = order_m + offset_k
    recurring = offset_k > 0.5
    beyond_one = offset_k > 1.5
    prior_degree = degree - 1.0
    factor_a = jnp.sqrt(
        jnp.where(recurring, 4.0 * degree * degree - 1.0, 1.0)
        / jnp.where(recurring, degree * degree - order_m * order_m, 1.0)
    )
    factor_b = jnp.sqrt(
        jnp.where(beyond_one, prior_degree * prior_degree - order_m * order_m, 0.0)
        / jnp.where(beyond_one, 4.0 * prior_degree * prior_degree - 1.0, 1.0)
    )
    log_start = 0.5 * (
        lax.lgamma(order_m + 1.5)
        - lax.lgamma(order_m + 1.0)
        - lax.lgamma(jnp.ones_like(order_m) * 1.5)
    ) + 0.5 * jnp.log(jnp.ones_like(order_m) * 0.5)
    factor_now = jnp.where(recurring & inside, factor_a, 0.0)
    factor_back = jnp.where(recurring & inside, -(factor_a * factor_b), 0.0)
    seed_mask = jnp.where(jnp.logical_not(recurring) & inside, 1.0, 0.0).astype(jnp.float32)
    log_cosine = jnp.log(1.0 - sines * sines)

    def to_blocks(table):
        return table.reshape(set_count, block_count, span_size).transpose(1, 0, 2)

    block_tables = (
        to_blocks(factor_now),
        to_blocks(factor_back),
        to_blocks(log_start),
        to_blocks(order_m),
        to_blocks(seed_mask),
    )

    def advance(carry, block_data):
        latest, earlier_value = carry
        now_table, back_table, start_table, order_table, mask_table = block_data
        produced = []
        for column in range(span_size):
            seed_value = mask_table[:, column : column + 1] * jnp.exp(
                start_table[:, column : column + 1]
                + 0.5 * order_table[:, column : column + 1] * log_cosine[None, :]
            )
            current = (
                now_table[:, column : column + 1] * sines[None, :] * latest
                + back_table[:, column : column + 1] * earlier_value
                + seed_value
            )
            earlier_value = latest
            latest = current
            produced.append(current)
        return ((latest, earlier_value), jnp.stack(produced, axis=2))

    zero_state = jnp.zeros((set_count, sines.shape[0]), jnp.float32)
    _, blocks_out = lax.scan(advance, (zero_state, zero_state), block_tables)
    result = blocks_out.transpose(1, 2, 0, 3).reshape(set_count, sines.shape[0], padded_length)
    return result[:, :, : M + 1]


def parity_weights(values, pairs, parity):
    slot_index = jnp.arange(NH, dtype=jnp.int32)[None, :]
    run_length = (M - pairs)[:, None]
    first_count = (run_length + 1 - parity) // 2
    second_count = (pairs[:, None] + 2 - parity) // 2
    source = jnp.where(
        slot_index < first_count,
        2 * slot_index + parity,
        run_length + 2 * (slot_index - first_count) + parity,
    )
    source = jnp.clip(source, 0, M)
    picked = jnp.take_along_axis(values, source[:, None, :], axis=2)
    in_first = (slot_index < first_count)[:, None, :]
    in_second = ((slot_index >= first_count) & (slot_index < first_count + second_count))[
        :, None, :
    ]
    return jnp.stack(
        [jnp.where(in_first, picked, 0.0), jnp.where(in_second, picked, 0.0)], axis=2
    ).astype(jnp.bfloat16)


def project(weights, coeffs):
    summed = jnp.einsum("stje,sec->tsjc", weights, coeffs, preferred_element_type=jnp.float32)
    return summed.astype(jnp.bfloat16)


def local(spectral, set_pair, lat_sines):
    half_lat = lax.axis_size("lat") // 2
    lat_index = lax.axis_index("lat")
    hemisphere = lat_index // half_lat
    band_index = lat_index % half_lat
    band_sines = lax.dynamic_slice_in_dim(lat_sines, band_index * BAND, BAND)
    sign_factor = (1 - 2 * hemisphere).astype(jnp.float32)
    values = legendre_runs(band_sines, set_pair)
    even_part = project(parity_weights(values, set_pair, 0), spectral[:, 0])
    odd_part = project(parity_weights(values, set_pair, 1), spectral[:, 1])
    even_part, odd_part = lax.optimization_barrier((even_part, odd_part))
    combined = (even_part.astype(jnp.float32) + sign_factor * odd_part.astype(jnp.float32)).astype(
        jnp.bfloat16
    )
    return lax.all_to_all(combined, "ma", split_axis=0, concat_axis=1, tiled=True)


def solution(mesh):
    placed = (P("ma", None, None, None), P("ma"), P())
    return jax.shard_map(
        local,
        mesh=mesh,
        in_specs=placed,
        out_specs=P(("lat", "ma"), None, None, None),
        check_vma=False,
    )
```

profile of v0, /device:TPU:1, one launch (start us, length us, event | category | flops | bytes accessed | tf_op | source)
XLA Modules:
  0.0 316.2 jit_solution(8106789208005886471)
XLA Ops:
  0.1 0.7 fusion.206
  0.7 0.1 and_bitcast_fusion
  0.8 0.1 bitcast_or_fusion
  1.2 0.7 fusion.157
  1.9 1.3 negate_select_fusion
  3.2 0.8 subtract_log_fusion
  4.0 146.7 %while.15 = (s32[]{:T(128)}, f32[8,80]{1,0:T(8,128)S(1)}, f32[8,80]{1,0:T(8,128)S(1)}, bf16[11,8,80,128]{2,1,3,0:T(8,128)(2,1)}, f32[11,8,128]{2,1,0:T(8,128)S(1...) while((s32[]{:T(128)}, f32[8,80]{1,0:T(8,128)S(1)}, ...), condition=%wide.region_1.2_spmd.clone, body=%wide.region_0.1_spmd.clone.sunk | while | flops 658306 | bytes 3099072 | solution.py:75
  4.0 0.1 copy.84
  4.3 0.1 copy.82
  4.5 0.1 copy.86
  4.8 0.1 copy.85
  5.0 0.1 copy.83
  16.6 0.7 bitcast_dynamic-update-slice_fusion.2
  17.4 0.1 copy.84
  17.9 0.1 copy.86
  18.1 0.1 copy.85
  18.4 0.1 copy.83
  30.0 0.7 bitcast_dynamic-update-slice_fusion.2
  30.7 0.1 copy.84
  31.0 0.1 copy.82
  31.2 0.1 copy.86
  31.5 0.1 copy.85
  31.7 0.1 copy.83
  43.3 0.7 bitcast_dynamic-update-slice_fusion.2
  44.0 0.1 copy.84
  44.3 0.1 copy.82
  44.5 0.1 copy.86
  44.8 0.1 copy.85
  45.0 0.1 copy.83
  56.6 0.7 bitcast_dynamic-update-slice_fusion.2
  57.4 0.1 copy.84
  57.6 0.1 copy.82
  57.9 0.1 copy.86
  58.1 0.1 copy.85
  70.0 0.7 bitcast_dynamic-update-slice_fusion.2
  70.7 0.1 copy.84
  83.3 0.7 bitcast_dynamic-update-slice_fusion.2
  84.0 0.1 copy.84
  96.6 0.7 bitcast_dynamic-update-slice_fusion.2
  97.4 0.1 copy.84
  110.0 0.8 bitcast_dynamic-update-slice_fusion.2
  110.7 0.1 copy.84
  123.3 0.7 bitcast_dynamic-update-slice_fusion.2
  124.1 0.1 copy.84
  136.7 0.7 bitcast_dynamic-update-slice_fusion.2
  137.4 0.1 copy.84
  150.0 0.7 bitcast_dynamic-update-slice_fusion.2
  150.7 1.8 slice.3216
  152.6 56.4 %gather_fusion.1 = bf16[5184,80]{1,0:T(8,128)(2,1)} fusion(bf16[8,80,1281]{1,0,2:T(8,128)(2,1)S(1)} %slice.3216, s32[5184]{0:T(1024)S(1)} %reshape.565), kind=kCustom, calls=%fused_computation.1.clone | custom fusion | bytes 1700352 | tf_op jit(solution)/shard_map/jit(take_along_axis)/gather | solution.py:91
  209.0 56.2 %gather_fusion = bf16[5184,80]{1,0:T(8,128)(2,1)} fusion(bf16[8,80,1281]{1,0,2:T(8,128)(2,1)S(1)} %slice.3216, s32[5184]{0:T(1024)S(1)} %reshape.560), kind=kCustom, calls=%fused_computation.clone | custom fusion | bytes 1700352 | tf_op jit(solution)/shard_map/jit(take_along_axis)/gather | solution.py:91
  265.1 1.7 copy.47
  266.9 1.4 copy.51
  268.4 1.7 fusion.155
  270.2 5.2 %convert_bitcast_fusion = bf16[80,8,2,768]{3,0,2,1:T(8,128)(2,1)S(1)} fusion(bf16[8,2,648,768]{3,2,1,0:T(8,128)(2,1)} %param.7, bf16[8,80,1,648]{3,1,0,2:T(8,128)(2,1)S(1)} %get-tuple-element.1044, bf16[8,80,1,648]{3,1,0,2:T(8,128)(2,1)S(1)} %get-tuple-element.1043), kind=kOutput, calls=%fused_computation.1055 | convolution fusion | flops 1275832320 | bytes 11587584 | tf_op jit(solution)/shard_map/stje,sec->tsjc/dot_general | solution.py:102
  275.4 0.5 fusion.153
  275.9 1.2 slice-done.2
  277.0 1.0 slice-done.3
  278.0 2.2 convert_bitcast_fusion.1
  280.2 0.6 add_convert_fusion
  280.8 1.5 copy.54
  282.4 29.9 %all_to_all.18 = bf16[80,8,2,768]{3,2,1,0:T(2,128)(2,1)S(1)} all-to-all(bf16[80,8,2,768]{3,2,1,0:T(2,128)(2,1)S(1)} %copy.54), channel_id=1, replica_groups=mesh['lat'=32,'ma'=8] {'ma'}, dimensions={0} | all-to-all | bytes 3932160 | tf_op jit(solution)/shard_map/all_to_all | solution.py:120
  312.3 0.3 copy.55
  312.6 0.2 copy.76
  312.8 3.3 %copy.57 = bf16[10,64,2,768]{3,2,1,0:T(2,128)(2,1)} copy(bf16[10,64,2,768]{3,1,2,0:T(8,128)(2,1)S(1)} %bitcast.1961) | data formatting | bytes 3932160 | tf_op jit(solution)/shard_map/all_to_all | solution.py:120
  (1870 shorter events, 132.3 us)
Async XLA Ops:
  265.1 1.8 copy-start
  270.1 5.8 %slice-start = ((s8[15925248]{0:T(1024)(128)(4,1)}), s8[4194304]{0:T(1024)(128)(4,1)S(1)}, s32[]{:S(2)}) async-start(s8[15925248]{0:T(1024)(128)(4,1)} %bitcast.2000), calls=%async_computation.1 | async-start | bytes 8388608
  270.1 5.8 %slice-start.1 = ((s8[15925248]{0:T(1024)(128)(4,1)}), s8[4194304]{0:T(1024)(128)(4,1)S(1)}, s32[]{:S(2)}) async-start(s8[15925248]{0:T(1024)(128)(4,1)} %bitcast.2000), calls=%async_computation.2 | async-start | bytes 8388608
  270.1 6.9 %slice-start.2 = ((s8[15925248]{0:T(1024)(128)(4,1)}), s8[4194304]{0:T(1024)(128)(4,1)S(1)}, s32[]{:S(2)}) async-start(s8[15925248]{0:T(1024)(128)(4,1)} %bitcast.2000), calls=%async_computation.3 | async-start | bytes 8388608
  270.1 7.9 %slice-start.3 = ((s8[15925248]{0:T(1024)(128)(4,1)}), s8[3342336]{0:T(1024)(128)(4,1)S(1)}, s32[]{:S(2)}) async-start(s8[15925248]{0:T(1024)(128)(4,1)} %bitcast.2000), calls=%async_computation.4 | async-start | bytes 6684672
where the time goes:
time: 317 us; the launch traced here: 316 us
  local copies, waits for them, and re-layouts  143 us (45%)
  other arithmetic  132 us (42%)
  blocking collectives  29.9 us (9%)
  matrix products  7.39 us (2%)
  loops' own time  3.68 us (1%)
    while x1397, other arithmetic  123 us
    gather x6, local copies, waits for them, and re-layouts, parity_weights(): picked = jnp.take_along_axis(values, source[:, None, :], axis=2)  116 us
    all_to_all x1, blocking collectives, local(): lax.all_to_all(combined, 'ma', split_axis=0, concat_axis=1, tiled=True)  29.9 us
    dynamic_update_slice x11, local copies, waits for them, and re-layouts, legendre_runs(): _, blocks_out = lax.scan(advance, (zero_state, zero_state), block_tables)  8.07 us
    dot_general x2, matrix products, project(): jnp.einsum('stje,sec->tsjc', weights, coeffs, preferred_element_type=jnp....  7.39 us

commit v1 on v0

v1 whole, which is shorter than its diff:
```python
import functools
import math

import jax
import jax.numpy as jnp
from jax import lax
from jax.experimental import pallas as pl
from jax.experimental.pallas import tpu as pltpu
from jax.sharding import PartitionSpec as P

M = 1280
NH = 648
COLS = 768
BAND = 80
ROWS = 10
SEG = 81
SETS = 4
MESH = pl.DeviceIdType.MESH
F32, BF16 = jnp.float32, jnp.bfloat16


def step_factors(pair):
    seg = lax.broadcasted_iota(jnp.int32, (8, 128), 0)
    lane = lax.broadcasted_iota(jnp.int32, (8, 128), 1)
    v = seg * SEG + lane
    split = (M + 1 - pair) // 2
    first = v < split
    order = jnp.where(first, pair, M - 1 - pair)
    offset = 2 * jnp.where(first, v, v - split)
    out = []
    for parity in range(2):
        k = (offset + parity).astype(F32)
        m = order.astype(F32)
        n = m + k
        num = 4.0 * n * n - 1.0
        den = k * (n + m)
        recurring = k > 0.5
        a = jnp.sqrt(jnp.where(recurring, num, 0.0) / jnp.where(recurring, den, 1.0))
        beyond = k > 1.5
        q = n - 1.0
        b = jnp.sqrt(
            jnp.where(beyond, (k - 1.0) * (q + m), 0.0)
            / jnp.where(beyond, 4.0 * q * q - 1.0, 1.0)
        )
        out += [a, -(a * b)]
    return out


def log_scale(order):
    k = (
        lax.broadcasted_iota(jnp.int32, (16, 128), 0) * 128
        + lax.broadcasted_iota(jnp.int32, (16, 128), 1)
        + 1
    )
    terms = jnp.log(1.0 + 0.5 / k.astype(F32))
    return 0.5 * (jnp.sum(jnp.where(k <= order, terms, 0.0)) - math.log(2.0))


def kernel(pair_ref, sines_ref, spec_ref, o_ref, spec, chain, weights, odd, sent, spec_sem, send_sem, recv_sem, own_sem):
    lat, ma = lax.axis_index("lat"), lax.axis_index("ma")
    core, x, y = lax.rem(lat, 2), ma // 2, lax.rem(ma, 2)
    base = lat - core
    sign = jnp.where(lat < 16, 1.0, -1.0).astype(F32)

    def load(s):
        return pltpu.make_async_copy(spec_ref.at[core * SETS + s], spec.at[s], spec_sem.at[s])

    for s in range(SETS):
        load(s).start()

    barrier = pltpu.get_barrier_semaphore()
    for c in range(2):
        for dx in range(4):
            for dy in range(2):
                to = (
                    base + (core if dx + dy == 0 else c),
                    lax.rem(x + dx, 4) * 2 + lax.rem(y + dy, 2),
                )
                if dx + dy > 0:
                    pl.semaphore_signal(barrier, inc=1, device_id=to, device_id_type=MESH)
    pl.semaphore_signal(barrier, inc=1, device_id=(base + 1 - core, ma), device_id_type=MESH)

    seg = lax.broadcasted_iota(jnp.int32, (8, 128), 0)
    lane = lax.broadcasted_iota(jnp.int32, (8, 128), 1)
    starts = seg * SEG
    sines, log_cos = [], []
    for c in range(2):
        at = lax.rem(base, 16) * BAND + c * BAND
        row, skip = at // 128, lax.rem(at, 128)
        here = jnp.broadcast_to(sines_ref[pl.ds(row, 1), :], (8, 128))
        after = jnp.broadcast_to(sines_ref[pl.ds(jnp.minimum(row + 1, 9), 1), :], (8, 128))
        turn = lax.rem(128 - skip, 128)
        value = jnp.where(lane < 128 - skip, pltpu.roll(here, turn, 1), pltpu.roll(after, turn, 1))
        sines.append(value)
        log_cos.append(jnp.log(1.0 - value * value))
        odd[c, pl.ds(NH, 8), :] = jnp.zeros((8, 128), F32)

    row = lax.broadcasted_iota(jnp.int32, (2 * BAND, 128), 0)
    col = lax.broadcasted_iota(jnp.int32, (2 * BAND, 128), 1)
    spread = (row // 2 == col).astype(BF16)

    def one_set(s, _):
        pair = pair_ref[core * SETS + s]
        split = (M + 1 - pair) // 2
        a_even, b_even, a_odd, b_odd = step_factors(pair)
        second = M - 1 - pair
        scale1, scale2 = log_scale(pair), log_scale(second)
        seeds1, seeds2 = [], []
        for c in range(2):
            seeds1.append(jnp.exp(scale1 + 0.5 * pair.astype(F32) * log_cos[c]))
            seeds2.append(jnp.exp(scale2 + 0.5 * second.astype(F32) * log_cos[c]))
        one, zero = jnp.ones((8, 128), F32), jnp.zeros((8, 128), F32)
        state = [[zero, one, one, zero] for c in range(2)]
        for k in range(SEG):
            ae = jnp.broadcast_to(a_even[:, k : k + 1], (8, 128))
            be = jnp.broadcast_to(b_even[:, k : k + 1], (8, 128))
            ao = jnp.broadcast_to(a_odd[:, k : k + 1], (8, 128))
            bo = jnp.broadcast_to(b_odd[:, k : k + 1], (8, 128))
            begins = starts == split - k
            for c in range(2):
                ue, uo, we, wo = state[c]
                axe, axo = ae * sines[c], ao * sines[c]
                ue = axe * uo + (be * ue + jnp.where(begins, seeds2[c], 0.0))
                if k == 0:
                    ue = jnp.where(seg == 0, seeds1[c], ue)
                we = axe * wo + be * we
                uo = axo * ue + bo * uo
                wo = axo * we + bo * wo
                state[c] = [ue, uo, we, wo]
                for i in range(4):
                    chain[c, i, k] = state[c][i]

        ahead = starts - split
        for c in range(2):
            alpha, beta = one, zero
            alphas, betas = one, zero
            for g in range(7):
                ends = [
                    jnp.broadcast_to(chain[c, i, SEG - 1, pl.ds(g, 1), :], (8, 128)) for i in range(4)
                ]
                turned = (g * SEG <= split) & (split < (g + 1) * SEG)
                alpha = jnp.where(turned, 1.0, alpha)
                alpha, beta = alpha * ends[1] + beta * ends[3], alpha * ends[0] + beta * ends[2]
                alphas = jnp.where(seg == g + 1, alpha, alphas)
                betas = jnp.where(seg == g + 1, beta, betas)
            for k in range(SEG):
                scale = jnp.where((ahead <= 0) & (ahead >= -k), 1.0, alphas)
                weights[c, pl.ds(k, 8, stride=SEG), :] = scale * chain[c, 0, k] + betas * chain[c, 2, k]
                odd[c, pl.ds(k, 8, stride=SEG), :] = scale * chain[c, 1, k] + betas * chain[c, 3, k]

        slot = lax.broadcasted_iota(jnp.int32, (NH, 128), 0)
        split_odd = (M - pair) // 2
        moved = slot >= jnp.where(lax.rem(pair, 2) == 1, split_odd, M)
        for c in range(2):
            picked = jnp.where(moved, odd[c, pl.ds(1, NH), :], odd[c, pl.ds(0, NH), :])
            weights[c, pl.ds(NH, NH), :] = sign * picked

        shape = (2 * BAND, 2 * NH)
        which = lax.rem(lax.broadcasted_iota(jnp.int32, shape, 0), 2)
        place = lax.broadcasted_iota(jnp.int32, shape, 1)
        even_part = place < NH
        slots = jnp.where(even_part, place, place - NH)
        cut = jnp.where(even_part, split, split_odd)
        total = jnp.where(even_part, M // 2 + 1, M // 2)
        low = jnp.where(which == 0, 0, cut)
        high = jnp.where(which == 0, cut, total)
        used = (slots >= low) & (slots < high)
        for c in range(2):
            wide = lax.dot_general(
                spread,
                weights[c].astype(BF16),
                (((1,), (1,)), ((), ())),
                preferred_element_type=F32,
            )
            lhs = jnp.where(used, wide, 0.0).astype(BF16)
            if c == 0:
                load(s).wait()
            summed = jnp.dot(lhs, spec[s], preferred_element_type=F32)
            unit = s * 2 + c
            sent[unit] = summed.astype(BF16).reshape(BAND, 2, COLS)
            if c == 0:

                @pl.when(s == 0)
                def _():
                    pl.semaphore_wait(barrier, 15)

            into = o_ref.at[:, ma * 8 + core * SETS + s]
            for dx in (2, 1, 3, 0):
                for dy in (1, 0):
                    to_ma = lax.rem(x + dx, 4) * 2 + lax.rem(y + dy, 2)
                    source = sent.at[unit, pl.ds(to_ma * ROWS, ROWS)]
                    remote = pltpu.make_async_remote_copy(
                        src_ref=source,
                        dst_ref=into,
                        send_sem=send_sem,
                        recv_sem=recv_sem,
                        device_id=(base + c, to_ma),
                        device_id_type=MESH,
                    )
                    if dx + dy > 0:
                        remote.start()
                    else:

                        @pl.when(core == c)
                        def _():
                            pltpu.make_async_copy(source, into, own_sem.at[s]).start()

                        @pl.when(core != c)
                        def _():
                            remote.start()

        return 0

    lax.fori_loop(0, SETS, one_set, 0)

    for s in range(SETS):
        pltpu.make_async_copy(sent.at[0, pl.ds(0, ROWS)], o_ref.at[:, 0], own_sem.at[s]).wait()
    most = o_ref.at[:, pl.ds(0, 60)]
    pltpu.make_async_copy(most, most, send_sem).wait()
    pltpu.make_async_copy(most, most, recv_sem).wait()


def local(spectral, set_pair, lat_sines):
    return pl.pallas_call(
        kernel,
        out_shape=jax.ShapeDtypeStruct((ROWS, 64, 2, COLS), BF16),
        in_specs=[
            pl.BlockSpec(memory_space=pltpu.SMEM),
            pl.BlockSpec(memory_space=pltpu.VMEM),
            pl.BlockSpec(memory_space=pl.ANY),
        ],
        out_specs=pl.BlockSpec(memory_space=pl.ANY),
        scratch_shapes=[
            pltpu.VMEM((SETS, 2 * NH, COLS), BF16),
            pltpu.VMEM((2, 4, SEG, 8, 128), F32),
            pltpu.VMEM((2, 2 * NH, 128), F32),
            pltpu.VMEM((2, NH + 8, 128), F32),
            pltpu.VMEM((2 * SETS, BAND, 2, COLS), BF16),
            pltpu.SemaphoreType.DMA((SETS,)),
            pltpu.SemaphoreType.DMA,
            pltpu.SemaphoreType.DMA,
            pltpu.SemaphoreType.DMA((SETS,)),
        ],
        compiler_params=pltpu.CompilerParams(
            collective_id=0, has_side_effects=True, vmem_limit_bytes=40 * 2**20
        ),
        cost_estimate=pl.CostEstimate(flops=2_600_000_000, bytes_accessed=12_000_000, transcendentals=0),
    )(set_pair, lat_sines.reshape(10, 128), spectral.reshape(8, 2 * NH, COLS))


def solution(mesh):
    placed = (P("ma", None, None, None), P("ma"), P())
    return jax.shard_map(
        local,
        mesh=mesh,
        in_specs=placed,
        out_specs=P(("lat", "ma"), None, None, None),
        check_vma=False,
    )
```

time: 317 us -> 31.9 us (0.10)
  local copies, waits for them, and re-layouts: 143 us -> 2.63 us
  other arithmetic: 132 us -> 0 us
  blocking collectives: 29.9 us -> 0 us
  Pallas kernels: 0 us -> 29.1 us
  matrix products: 7.39 us -> 0 us
  loops' own time: 3.68 us -> 0 us
    while x1397 -> x0, other arithmetic: 123 us -> none
    gather x6 -> x0, local copies, waits for them, and re-layouts: 116 us -> none  [parity_weights(): picked = jnp.take_along_axis(values, source[:, None, :], axis=2)]
    all_to_all x1 -> x0, blocking collectives: 29.9 us -> none  [local(): lax.all_to_all(combined, 'ma', split_axis=0, concat_axis=1, tiled=True)]
    pallas_call x0 -> x1, Pallas kernels: none -> 29.1 us  [local(): pl.pallas_call(kernel, out_shape=jax.ShapeDtypeStruct((ROWS, 64, 2, COLS)...]
    dynamic_update_slice x11 -> x0, local copies, waits for them, and re-layouts: 8.07 us -> none  [legendre_runs(): _, blocks_out = lax.scan(advance, (zero_state, zero_state), block_tables)]
    dot_general x2 -> x0, matrix products: 7.39 us -> none  [project(): jnp.einsum('stje,sec->tsjc', weights, coeffs, preferred_element_type=jnp....]
    dynamic_slice x88 -> x0, local copies, waits for them, and re-layouts: 5.67 us -> none  [legendre_runs(): _, blocks_out = lax.scan(advance, (zero_state, zero_state), block_tables)]
    all_to_all x3 -> x0, local copies, waits for them, and re-layouts: 3.84 us -> none  [local(): lax.all_to_all(combined, 'ma', split_axis=0, concat_axis=1, tiled=True)]
where the time goes in v1:
time: 31.9 us; the launch traced here: 31.8 us
  Pallas kernels  29.1 us (91%)
  local copies, waits for them, and re-layouts  2.63 us (8%)
    pallas_call x1, Pallas kernels, local(): pl.pallas_call(kernel, out_shape=jax.ShapeDtypeStruct((ROWS, 64, 2, COLS)...  29.1 us
    unnamed x5, local copies, waits for them, and re-layouts  2.63 us

profile of v1, /device:TPU:1, one launch (start us, length us, event | category | flops | bytes accessed | tf_op | source)
XLA Modules:
  0.0 31.8 jit_solution(4017783922637705628)
XLA Ops:
  0.0 0.0 copy-start
  0.0 0.7 %copy-done = f32[1280]{0:T(1024)S(1)} copy-done((f32[1280]{0:T(1024)S(1)}, f32[1280]{0:T(1024)}, u32[]{:S(2)}) %copy-start) | copy-done | bytes 5144
  0.7 0.0 copy-start.1
  0.7 0.7 %copy-done.1 = s32[8]{0:T(128)S(1)} copy-done((s32[8]{0:T(128)S(1)}, s32[8]{0:T(128)}, u32[]{:S(2)}) %copy-start.1) | copy-done | bytes 56
  1.4 29.1 %shard_map.37 = bf16[10,64,2,768]{3,2,1,0:T(2,128)(2,1)S(1)} custom-call(s32[8]{0:T(128)S(1)} %copy-done.1, f32[10,128]{1,0:T(8,128)S(1)} %bitcast.2, bf16[8,1296,768]{2,1,0:T(8,128)(2,1)} %bitcast.3), custom_call_target="tpu_custom_call" | custom-call | flops 2600000000 | bytes 12000000 | tf_op jit(solution)/shard_map/pallas_call | solution.py:224
  30.5 1.3 %copy.5 = bf16[10,64,2,768]{3,2,1,0:T(2,128)(2,1)} copy(bf16[10,64,2,768]{3,2,1,0:T(2,128)(2,1)S(1)} %shard_map.37) | data formatting | bytes 3932160
Async XLA Ops:
  0.0 0.7 %copy-start = (f32[1280]{0:T(1024)S(1)}, f32[1280]{0:T(1024)}, u32[]{:S(2)}) copy-start(f32[1280]{0:T(1024)} %param.5) | copy-start | bytes 15364
  0.7 0.7 %copy-start.1 = (s32[8]{0:T(128)S(1)}, s32[8]{0:T(128)}, u32[]{:S(2)}) copy-start(s32[8]{0:T(128)} %pair_ref.1) | copy-start | bytes 100

commit v2 on v1

--- a/solution.py
+++ b/solution.py
@@ -16,6 +16,8 @@
 SEG = 81
 SETS = 4
 MESH = pl.DeviceIdType.MESH
+ORDER = [(dx, dy) for dx in (2, 1, 3, 0) for dy in (1, 0)]
+CUTS = 2
 F32, BF16 = jnp.float32, jnp.bfloat16
 
 
@@ -56,7 +58,9 @@
     return 0.5 * (jnp.sum(jnp.where(k <= order, terms, 0.0)) - math.log(2.0))
 
 
-def kernel(pair_ref, sines_ref, spec_ref, o_ref, spec, chain, weights, odd, sent, spec_sem, send_sem, recv_sem, own_sem):
+def kernel(
+    pairs_ref, lats_ref, spec_ref, o_ref, pair_ref, sines_ref, spec, chain, weights, odd, sent, small_sem, spec_sem, send_sem, recv_sem, own_sem
+):
     lat, ma = lax.axis_index("lat"), lax.axis_index("ma")
     core, x, y = lax.rem(lat, 2), ma // 2, lax.rem(ma, 2)
     base = lat - core
@@ -65,8 +69,13 @@
     def load(s):
         return pltpu.make_async_copy(spec_ref.at[core * SETS + s], spec.at[s], spec_sem.at[s])
 
-    for s in range(SETS):
-        load(s).start()
+    small = [
+        pltpu.make_async_copy(pairs_ref, pair_ref, small_sem.at[0]),
+        pltpu.make_async_copy(lats_ref, sines_ref, small_sem.at[1]),
+    ]
+    for copy in small:
+        copy.start()
+    load(0).start()
 
     barrier = pltpu.get_barrier_semaphore()
     for c in range(2):
@@ -80,6 +89,8 @@
                     pl.semaphore_signal(barrier, inc=1, device_id=to, device_id_type=MESH)
     pl.semaphore_signal(barrier, inc=1, device_id=(base + 1 - core, ma), device_id_type=MESH)
 
+    for copy in small:
+        copy.wait()
     seg = lax.broadcasted_iota(jnp.int32, (8, 128), 0)
     lane = lax.broadcasted_iota(jnp.int32, (8, 128), 1)
     starts = seg * SEG
@@ -97,7 +108,11 @@
 
     row = lax.broadcasted_iota(jnp.int32, (2 * BAND, 128), 0)
     col = lax.broadcasted_iota(jnp.int32, (2 * BAND, 128), 1)
-    spread = (row // 2 == col).astype(BF16)
+    place = jnp.zeros((2 * BAND, 128), jnp.int32)
+    for d, (dx, dy) in enumerate(ORDER):
+        to_ma = lax.rem(x + dx, 4) * 2 + lax.rem(y + dy, 2)
+        place = jnp.where(row >= d * 2 * ROWS, to_ma * ROWS - d * ROWS, place)
+    spread = (row // 2 + place == col).astype(BF16)
 
     def one_set(s, _):
         pair = pair_ref[core * SETS + s]
@@ -175,20 +190,31 @@
             lhs = jnp.where(used, wide, 0.0).astype(BF16)
             if c == 0:
                 load(s).wait()
-            summed = jnp.dot(lhs, spec[s], preferred_element_type=F32)
+
+                @pl.when(s + 1 < SETS)
+                def _():
+                    load(s + 1).start()
+
             unit = s * 2 + c
-            sent[unit] = summed.astype(BF16).reshape(BAND, 2, COLS)
-            if c == 0:
-
-                @pl.when(s == 0)
-                def _():
-                    pl.semaphore_wait(barrier, 15)
-
             into = o_ref.at[:, ma * 8 + core * SETS + s]
-            for dx in (2, 1, 3, 0):
-                for dy in (1, 0):
+            height = 2 * BAND // CUTS
+            for h in range(CUTS):
+                summed = jnp.dot(
+                    lhs[h * height : (h + 1) * height], spec[s], preferred_element_type=F32
+                )
+                sent[unit, pl.ds(h * height // 2, height // 2)] = summed.astype(BF16).reshape(
+                    height // 2, 2, COLS
+                )
+                if c == 0 and h == 0:
+
+                    @pl.when(s == 0)
+                    def _():
+                        pl.semaphore_wait(barrier, 15)
+
+                for d in range(h * 8 // CUTS, (h + 1) * 8 // CUTS):
+                    dx, dy = ORDER[d]
                     to_ma = lax.rem(x + dx, 4) * 2 + lax.rem(y + dy, 2)
-                    source = sent.at[unit, pl.ds(to_ma * ROWS, ROWS)]
+                    source = sent.at[unit, pl.ds(d * ROWS, ROWS)]
                     remote = pltpu.make_async_remote_copy(
                         src_ref=source,
                         dst_ref=into,
@@ -220,22 +246,29 @@
     pltpu.make_async_copy(most, most, recv_sem).wait()
 
 
+def in_hbm(array):
+    return pltpu.with_memory_space_constraint(array, pltpu.HBM)
+
+
 def local(spectral, set_pair, lat_sines):
     return pl.pallas_call(
         kernel,
         out_shape=jax.ShapeDtypeStruct((ROWS, 64, 2, COLS), BF16),
         in_specs=[
-            pl.BlockSpec(memory_space=pltpu.SMEM),
-            pl.BlockSpec(memory_space=pltpu.VMEM),
+            pl.BlockSpec(memory_space=pltpu.HBM),
+            pl.BlockSpec(memory_space=pltpu.HBM),
             pl.BlockSpec(memory_space=pl.ANY),
         ],
         out_specs=pl.BlockSpec(memory_space=pl.ANY),
         scratch_shapes=[
+            pltpu.SMEM((8,), jnp.int32),
+            pltpu.VMEM((10, 128), F32),
             pltpu.VMEM((SETS, 2 * NH, COLS), BF16),
             pltpu.VMEM((2, 4, SEG, 8, 128), F32),
             pltpu.VMEM((2, 2 * NH, 128), F32),
             pltpu.VMEM((2, NH + 8, 128), F32),
             pltpu.VMEM((2 * SETS, BAND, 2, COLS), BF16),
+            pltpu.SemaphoreType.DMA((2,)),
             pltpu.SemaphoreType.DMA((SETS,)),
             pltpu.SemaphoreType.DMA,
             pltpu.SemaphoreType.DMA,
@@ -245,7 +278,7 @@
             collective_id=0, has_side_effects=True, vmem_limit_bytes=40 * 2**20
         ),
         cost_estimate=pl.CostEstimate(flops=2_600_000_000, bytes_accessed=12_000_000, transcendentals=0),
-    )(set_pair, lat_sines.reshape(10, 128), spectral.reshape(8, 2 * NH, COLS))
+    )(in_hbm(set_pair), in_hbm(lat_sines.reshape(10, 128)), spectral.reshape(8, 2 * NH, COLS))
 
 
 def solution(mesh):

time: 31.9 us -> 30.1 us (0.944)
  local copies, waits for them, and re-layouts: 2.63 us -> 1.27 us
  Pallas kernels: 29.1 us -> 28.7 us
    unnamed x5 -> x1, local copies, waits for them, and re-layouts: 2.63 us -> 1.27 us
    pallas_call x1, Pallas kernels: 29.1 us -> 28.7 us  [local(): pl.pallas_call(kernel, out_shape=jax.ShapeDtypeStruct((ROWS, 64, 2, COLS)...]
where the time goes in v2:
time: 30.1 us; the launch traced here: 30 us
  Pallas kernels  28.7 us (95%)
  local copies, waits for them, and re-layouts  1.27 us (4%)
    pallas_call x1, Pallas kernels, local(): pl.pallas_call(kernel, out_shape=jax.ShapeDtypeStruct((ROWS, 64, 2, COLS)...  28.7 us
    unnamed x1, local copies, waits for them, and re-layouts  1.27 us

profile of v2, /device:TPU:1, one launch (start us, length us, event | category | flops | bytes accessed | tf_op | source)
XLA Modules:
  0.0 30.0 jit_solution(6955861466357468842)
XLA Ops:
  0.0 28.7 %shard_map.37 = bf16[10,64,2,768]{3,2,1,0:T(2,128)(2,1)S(1)} custom-call(s32[8]{0:T(128)} %pairs_ref.1, f32[10,128]{1,0:T(8,128)} %bitcast.3, bf16[8,1296,768]{2,1,0:T(8,128)(2,1)} %bitcast.2), custom_call_target="tpu_custom_call" | custom-call | flops 2600000000 | bytes 12000000 | tf_op jit(solution)/shard_map/pallas_call | solution.py:254
  28.7 1.3 %copy.5 = bf16[10,64,2,768]{3,2,1,0:T(2,128)(2,1)} copy(bf16[10,64,2,768]{3,2,1,0:T(2,128)(2,1)S(1)} %shard_map.37) | data formatting | bytes 3932160

commit v3 on v2

v3 whole, which is shorter than its diff:
```python
import functools
import math

import jax
import jax.numpy as jnp
from jax import lax
from jax.experimental import pallas as pl
from jax.experimental.pallas import tpu as pltpu
from jax.sharding import PartitionSpec as P

M = 1280
NH = 648
COLS = 768
BAND = 80
ROWS = 10
SEG = 81
SETS = 8
MESH = pl.DeviceIdType.MESH
ORDER = [(dx, dy) for dx in (2, 1, 3, 0) for dy in (1, 0)]
CUTS = 2
F32, BF16 = jnp.float32, jnp.bfloat16


def step_factors(pair):
    seg = lax.broadcasted_iota(jnp.int32, (8, 128), 0)
    lane = lax.broadcasted_iota(jnp.int32, (8, 128), 1)
    v = seg * SEG + lane
    split = (M + 1 - pair) // 2
    first = v < split
    order = jnp.where(first, pair, M - 1 - pair)
    offset = 2 * jnp.where(first, v, v - split)
    out = []
    for parity in range(2):
        k = (offset + parity).astype(F32)
        m = order.astype(F32)
        n = m + k
        num = 4.0 * n * n - 1.0
        den = k * (n + m)
        recurring = k > 0.5
        a = jnp.sqrt(jnp.where(recurring, num, 0.0) / jnp.where(recurring, den, 1.0))
        beyond = k > 1.5
        q = n - 1.0
        b = jnp.sqrt(
            jnp.where(beyond, (k - 1.0) * (q + m), 0.0)
            / jnp.where(beyond, 4.0 * q * q - 1.0, 1.0)
        )
        out += [a, -(a * b)]
    return out


def log_scale(order):
    k = (
        lax.broadcasted_iota(jnp.int32, (16, 128), 0) * 128
        + lax.broadcasted_iota(jnp.int32, (16, 128), 1)
        + 1
    )
    terms = jnp.log(1.0 + 0.5 / k.astype(F32))
    return 0.5 * (jnp.sum(jnp.where(k <= order, terms, 0.0)) - math.log(2.0))


def kernel(
    pairs_ref, lats_ref, spec_ref, o_ref, pair_ref, sines_ref, spec, chain, weights, odd, sent, small_sem, spec_sem, send_sem, recv_sem, own_sem
):
    lat, ma = lax.axis_index("lat"), lax.axis_index("ma")
    x, y = ma // 2, lax.rem(ma, 2)
    sign = jnp.where(lat < 16, 1.0, -1.0).astype(F32)

    def load(s):
        return pltpu.make_async_copy(spec_ref.at[s], spec.at[s], spec_sem.at[s])

    small = [
        pltpu.make_async_copy(pairs_ref, pair_ref, small_sem.at[0]),
        pltpu.make_async_copy(lats_ref, sines_ref, small_sem.at[1]),
    ]
    for copy in small:
        copy.start()
    load(0).start()

    barrier = pltpu.get_barrier_semaphore()
    for dx, dy in ORDER[:-1]:
        to = (lat, lax.rem(x + dx, 4) * 2 + lax.rem(y + dy, 2))
        pl.semaphore_signal(barrier, inc=1, device_id=to, device_id_type=MESH)

    for copy in small:
        copy.wait()
    seg = lax.broadcasted_iota(jnp.int32, (8, 128), 0)
    lane = lax.broadcasted_iota(jnp.int32, (8, 128), 1)
    starts = seg * SEG
    at = lax.rem(lat, 16) * BAND
    row, skip = at // 128, lax.rem(at, 128)
    here = jnp.broadcast_to(sines_ref[pl.ds(row, 1), :], (8, 128))
    after = jnp.broadcast_to(sines_ref[pl.ds(jnp.minimum(row + 1, 9), 1), :], (8, 128))
    turn = lax.rem(128 - skip, 128)
    sines = jnp.where(lane < 128 - skip, pltpu.roll(here, turn, 1), pltpu.roll(after, turn, 1))
    log_cos = jnp.log(1.0 - sines * sines)
    odd[pl.ds(NH, 8), :] = jnp.zeros((8, 128), F32)

    row = lax.broadcasted_iota(jnp.int32, (2 * BAND, 128), 0)
    col = lax.broadcasted_iota(jnp.int32, (2 * BAND, 128), 1)
    place = jnp.zeros((2 * BAND, 128), jnp.int32)
    for d, (dx, dy) in enumerate(ORDER):
        to_ma = lax.rem(x + dx, 4) * 2 + lax.rem(y + dy, 2)
        place = jnp.where(row >= d * 2 * ROWS, to_ma * ROWS - d * ROWS, place)
    spread = (row // 2 + place == col).astype(BF16)

    def one_set(s, _):
        pair = pair_ref[s]
        split = (M + 1 - pair) // 2
        a_even, b_even, a_odd, b_odd = step_factors(pair)
        second = M - 1 - pair
        seed1 = jnp.exp(log_scale(pair) + 0.5 * pair.astype(F32) * log_cos)
        seed2 = jnp.exp(log_scale(second) + 0.5 * second.astype(F32) * log_cos)
        one, zero = jnp.ones((8, 128), F32), jnp.zeros((8, 128), F32)
        ue, uo, we, wo = zero, one, one, zero
        for k in range(SEG):
            ae = jnp.broadcast_to(a_even[:, k : k + 1], (8, 128)) * sines
            be = jnp.broadcast_to(b_even[:, k : k + 1], (8, 128))
            ao = jnp.broadcast_to(a_odd[:, k : k + 1], (8, 128)) * sines
            bo = jnp.broadcast_to(b_odd[:, k : k + 1], (8, 128))
            ue = ae * uo + (be * ue + jnp.where(starts == split - k, seed2, 0.0))
            if k == 0:
                ue = jnp.where(seg == 0, seed1, ue)
            we = ae * wo + be * we
            uo = ao * ue + bo * uo
            wo = ao * we + bo * wo
            for i, value in enumerate((ue, uo, we, wo)):
                chain[i, k] = value

        ahead = starts - split
        alpha, beta = one, zero
        alphas, betas = one, zero
        for g in range(7):
            ends = [jnp.broadcast_to(chain[i, SEG - 1, pl.ds(g, 1), :], (8, 128)) for i in range(4)]
            turned = (g * SEG <= split) & (split < (g + 1) * SEG)
            alpha = jnp.where(turned, 1.0, alpha)
            alpha, beta = alpha * ends[1] + beta * ends[3], alpha * ends[0] + beta * ends[2]
            alphas = jnp.where(seg == g + 1, alpha, alphas)
            betas = jnp.where(seg == g + 1, beta, betas)
        for k in range(SEG):
            scale = jnp.where((ahead <= 0) & (ahead >= -k), 1.0, alphas)
            weights[pl.ds(k, 8, stride=SEG), :] = scale * chain[0, k] + betas * chain[2, k]
            odd[pl.ds(k, 8, stride=SEG), :] = scale * chain[1, k] + betas * chain[3, k]

        slot = lax.broadcasted_iota(jnp.int32, (NH, 128), 0)
        split_odd = (M - pair) // 2
        moved = slot >= jnp.where(lax.rem(pair, 2) == 1, split_odd, M)
        picked = jnp.where(moved, odd[pl.ds(1, NH), :], odd[pl.ds(0, NH), :])
        weights[pl.ds(NH, NH), :] = sign * picked

        shape = (2 * BAND, 2 * NH)
        which = lax.rem(lax.broadcasted_iota(jnp.int32, shape, 0), 2)
        place = lax.broadcasted_iota(jnp.int32, shape, 1)
        even_part = place < NH
        slots = jnp.where(even_part, place, place - NH)
        cut = jnp.where(even_part, split, split_odd)
        total = jnp.where(even_part, M // 2 + 1, M // 2)
        low = jnp.where(which == 0, 0, cut)
        high = jnp.where(which == 0, cut, total)
        used = (slots >= low) & (slots < high)
        wide = lax.dot_general(
            spread, weights[...].astype(BF16), (((1,), (1,)), ((), ())), preferred_element_type=F32
        )
        lhs = jnp.where(used, wide, 0.0).astype(BF16)
        load(s).wait()

        @pl.when(s + 1 < SETS)
        def _():
            load(s + 1).start()

        into = o_ref.at[:, ma * 8 + s]
        height = 2 * BAND // CUTS
        for h in range(CUTS):
            summed = jnp.dot(lhs[h * height : (h + 1) * height], spec[s], preferred_element_type=F32)
            sent[s, pl.ds(h * height // 2, height // 2)] = summed.astype(BF16).reshape(
                height // 2, 2, COLS
            )
            if h == 0:

                @pl.when(s == 0)
                def _():
                    pl.semaphore_wait(barrier, 7)

            for d in range(h * 8 // CUTS, (h + 1) * 8 // CUTS):
                dx, dy = ORDER[d]
                source = sent.at[s, pl.ds(d * ROWS, ROWS)]
                if dx + dy > 0:
                    pltpu.make_async_remote_copy(
                        src_ref=source,
                        dst_ref=into,
                        send_sem=send_sem,
                        recv_sem=recv_sem,
                        device_id=(lat, lax.rem(x + dx, 4) * 2 + lax.rem(y + dy, 2)),
                        device_id_type=MESH,
                    ).start()
                else:
                    pltpu.make_async_copy(source, into, own_sem.at[s]).start()
        return 0

    lax.fori_loop(0, SETS, one_set, 0)

    for s in range(SETS):
        pltpu.make_async_copy(sent.at[0, pl.ds(0, ROWS)], o_ref.at[:, 0], own_sem.at[s]).wait()
    most = o_ref.at[:, pl.ds(0, 56)]
    pltpu.make_async_copy(most, most, send_sem).wait()
    pltpu.make_async_copy(most, most, recv_sem).wait()


def in_hbm(array):
    return pltpu.with_memory_space_constraint(array, pltpu.HBM)


def local(spectral, set_pair, lat_sines):
    return pl.pallas_call(
        kernel,
        out_shape=jax.ShapeDtypeStruct((ROWS, 64, 2, COLS), BF16),
        in_specs=[
            pl.BlockSpec(memory_space=pltpu.HBM),
            pl.BlockSpec(memory_space=pltpu.HBM),
            pl.BlockSpec(memory_space=pl.ANY),
        ],
        out_specs=pl.BlockSpec(memory_space=pl.ANY),
        scratch_shapes=[
            pltpu.SMEM((8,), jnp.int32),
            pltpu.VMEM((10, 128), F32),
            pltpu.VMEM((SETS, 2 * NH, COLS), BF16),
            pltpu.VMEM((4, SEG, 8, 128), F32),
            pltpu.VMEM((2 * NH, 128), F32),
            pltpu.VMEM((NH + 8, 128), F32),
            pltpu.VMEM((SETS, BAND, 2, COLS), BF16),
            pltpu.SemaphoreType.DMA((2,)),
            pltpu.SemaphoreType.DMA((SETS,)),
            pltpu.SemaphoreType.DMA,
            pltpu.SemaphoreType.DMA,
            pltpu.SemaphoreType.DMA((SETS,)),
        ],
        compiler_params=pltpu.CompilerParams(
            collective_id=0, has_side_effects=True, vmem_limit_bytes=40 * 2**20
        ),
        cost_estimate=pl.CostEstimate(flops=2_600_000_000, bytes_accessed=20_000_000, transcendentals=0),
    )(in_hbm(set_pair), in_hbm(lat_sines.reshape(10, 128)), spectral.reshape(8, 2 * NH, COLS))


def solution(mesh):
    placed = (P("ma", None, None, None), P("ma"), P())
    return jax.shard_map(
        local,
        mesh=mesh,
        in_specs=placed,
        out_specs=P(("lat", "ma"), None, None, None),
        check_vma=False,
    )
```

time: 30.1 us -> 29.3 us (0.973)
  Pallas kernels: 28.7 us -> 27.9 us
    pallas_call x1, Pallas kernels: 28.7 us -> 27.9 us  [local(): pl.pallas_call(kernel, out_shape=jax.ShapeDtypeStruct((ROWS, 64, 2, COLS)...]
where the time goes in v3:
time: 29.3 us; the launch traced here: 29.2 us
  Pallas kernels  27.9 us (95%)
  local copies, waits for them, and re-layouts  1.27 us (4%)
    pallas_call x1, Pallas kernels, local(): pl.pallas_call(kernel, out_shape=jax.ShapeDtypeStruct((ROWS, 64, 2, COLS)...  27.9 us
    unnamed x1, local copies, waits for them, and re-layouts  1.27 us

profile of v3, /device:TPU:1, one launch (start us, length us, event | category | flops | bytes accessed | tf_op | source)
XLA Modules:
  0.0 29.2 jit_solution(748949771268332167)
XLA Ops:
  0.0 27.9 %shard_map.37 = bf16[10,64,2,768]{3,2,1,0:T(2,128)(2,1)S(1)} custom-call(s32[8]{0:T(128)} %pairs_ref.1, f32[10,128]{1,0:T(8,128)} %bitcast.3, bf16[8,1296,768]{2,1,0:T(8,128)(2,1)} %bitcast.2), custom_call_target="tpu_custom_call" | custom-call | flops 2600000000 | bytes 20000000 | tf_op jit(solution)/shard_map/pallas_call | solution.py:213
  27.9 1.3 %copy.5 = bf16[10,64,2,768]{3,2,1,0:T(2,128)(2,1)} copy(bf16[10,64,2,768]{3,2,1,0:T(2,128)(2,1)S(1)} %shard_map.37) | data formatting | bytes 3932160

commit v4 on v3

--- a/solution.py
+++ b/solution.py
@@ -48,13 +48,17 @@
     return out
 
 
-def log_scale(order):
+def log_terms():
     k = (
         lax.broadcasted_iota(jnp.int32, (16, 128), 0) * 128
         + lax.broadcasted_iota(jnp.int32, (16, 128), 1)
         + 1
     )
-    terms = jnp.log(1.0 + 0.5 / k.astype(F32))
+    return k, jnp.log(1.0 + 0.5 / k.astype(F32))
+
+
+def log_scale(table, order):
+    k, terms = table
     return 0.5 * (jnp.sum(jnp.where(k <= order, terms, 0.0)) - math.log(2.0))
 
 
@@ -80,6 +84,17 @@
     for dx, dy in ORDER[:-1]:
         to = (lat, lax.rem(x + dx, 4) * 2 + lax.rem(y + dy, 2))
         pl.semaphore_signal(barrier, inc=1, device_id=to, device_id_type=MESH)
+
+    row = lax.broadcasted_iota(jnp.int32, (2 * BAND, 128), 0)
+    col = lax.broadcasted_iota(jnp.int32, (2 * BAND, 128), 1)
+    place = jnp.zeros((2 * BAND, 128), jnp.int32)
+    for d, (dx, dy) in enumerate(ORDER):
+        to_ma = lax.rem(x + dx, 4) * 2 + lax.rem(y + dy, 2)
+        place = jnp.where(row >= d * 2 * ROWS, to_ma * ROWS - d * ROWS, place)
+    spread = (row // 2 + place == col).astype(BF16)
+    table = log_terms()
+    which = lax.broadcasted_iota(jnp.int32, (8, 2 * NH), 0) & 1
+    column = lax.broadcasted_iota(jnp.int32, (8, 2 * NH), 1)
 
     for copy in small:
         copy.wait()
@@ -95,21 +110,11 @@
     log_cos = jnp.log(1.0 - sines * sines)
     odd[pl.ds(NH, 8), :] = jnp.zeros((8, 128), F32)
 
-    row = lax.broadcasted_iota(jnp.int32, (2 * BAND, 128), 0)
-    col = lax.broadcasted_iota(jnp.int32, (2 * BAND, 128), 1)
-    place = jnp.zeros((2 * BAND, 128), jnp.int32)
-    for d, (dx, dy) in enumerate(ORDER):
-        to_ma = lax.rem(x + dx, 4) * 2 + lax.rem(y + dy, 2)
-        place = jnp.where(row >= d * 2 * ROWS, to_ma * ROWS - d * ROWS, place)
-    spread = (row // 2 + place == col).astype(BF16)
-
     def one_set(s, _):
         pair = pair_ref[s]
         split = (M + 1 - pair) // 2
         a_even, b_even, a_odd, b_odd = step_factors(pair)
         second = M - 1 - pair
-        seed1 = jnp.exp(log_scale(pair) + 0.5 * pair.astype(F32) * log_cos)
-        seed2 = jnp.exp(log_scale(second) + 0.5 * second.astype(F32) * log_cos)
         one, zero = jnp.ones((8, 128), F32), jnp.zeros((8, 128), F32)
         ue, uo, we, wo = zero, one, one, zero
         for k in range(SEG):
@@ -117,27 +122,29 @@
             be = jnp.broadcast_to(b_even[:, k : k + 1], (8, 128))
             ao = jnp.broadcast_to(a_odd[:, k : k + 1], (8, 128)) * sines
             bo = jnp.broadcast_to(b_odd[:, k : k + 1], (8, 128))
-            ue = ae * uo + (be * ue + jnp.where(starts == split - k, seed2, 0.0))
+            ue = ae * uo + (be * ue + jnp.where(starts == split - k, 1.0, 0.0))
             if k == 0:
-                ue = jnp.where(seg == 0, seed1, ue)
+                ue = jnp.where(seg == 0, 1.0, ue)
             we = ae * wo + be * we
             uo = ao * ue + bo * uo
             wo = ao * we + bo * wo
             for i, value in enumerate((ue, uo, we, wo)):
                 chain[i, k] = value
 
+        seed1 = jnp.exp(log_scale(table, pair) + 0.5 * pair.astype(F32) * log_cos)
+        seed2 = jnp.exp(log_scale(table, second) + 0.5 * second.astype(F32) * log_cos)
         ahead = starts - split
-        alpha, beta = one, zero
-        alphas, betas = one, zero
+        alpha, beta = seed1, zero
+        alphas, betas = seed1, zero
         for g in range(7):
             ends = [jnp.broadcast_to(chain[i, SEG - 1, pl.ds(g, 1), :], (8, 128)) for i in range(4)]
             turned = (g * SEG <= split) & (split < (g + 1) * SEG)
-            alpha = jnp.where(turned, 1.0, alpha)
+            alpha = jnp.where(turned, seed2, alpha)
             alpha, beta = alpha * ends[1] + beta * ends[3], alpha * ends[0] + beta * ends[2]
             alphas = jnp.where(seg == g + 1, alpha, alphas)
             betas = jnp.where(seg == g + 1, beta, betas)
         for k in range(SEG):
-            scale = jnp.where((ahead <= 0) & (ahead >= -k), 1.0, alphas)
+            scale = jnp.where((ahead <= 0) & (ahead >= -k), seed2, alphas)
             weights[pl.ds(k, 8, stride=SEG), :] = scale * chain[0, k] + betas * chain[2, k]
             odd[pl.ds(k, 8, stride=SEG), :] = scale * chain[1, k] + betas * chain[3, k]
 
@@ -147,11 +154,8 @@
         picked = jnp.where(moved, odd[pl.ds(1, NH), :], odd[pl.ds(0, NH), :])
         weights[pl.ds(NH, NH), :] = sign * picked
 
-        shape = (2 * BAND, 2 * NH)
-        which = lax.rem(lax.broadcasted_iota(jnp.int32, shape, 0), 2)
-        place = lax.broadcasted_iota(jnp.int32, shape, 1)
-        even_part = place < NH
-        slots = jnp.where(even_part, place, place - NH)
+        even_part = column < NH
+        slots = jnp.where(even_part, column, column - NH)
         cut = jnp.where(even_part, split, split_odd)
         total = jnp.where(even_part, M // 2 + 1, M // 2)
         low = jnp.where(which == 0, 0, cut)
@@ -160,7 +164,8 @@
         wide = lax.dot_general(
             spread, weights[...].astype(BF16), (((1,), (1,)), ((), ())), preferred_element_type=F32
         )
-        lhs = jnp.where(used, wide, 0.0).astype(BF16)
+        lhs = jnp.where(used[None], wide.reshape(2 * BAND // 8, 8, 2 * NH), 0.0)
+        lhs = lhs.reshape(2 * BAND, 2 * NH).astype(BF16)
         load(s).wait()
 
         @pl.when(s + 1 < SETS)

time: 29.3 us -> 29.2 us (level)
  no operation moved by 1% of the time
where the time goes in v4:
time: 29.2 us
  Pallas kernels  27.9 us (96%)
  local copies, waits for them, and re-layouts  1.27 us (4%)
    pallas_call x1, Pallas kernels, local(): pl.pallas_call(kernel, out_shape=jax.ShapeDtypeStruct((ROWS, 64, 2, COLS)...  27.9 us
    unnamed x1, local copies, waits for them, and re-layouts  1.27 us

profile of v4, /device:TPU:1, one launch (start us, length us, event | category | flops | bytes accessed | tf_op | source)
XLA Modules:
  0.0 29.2 jit_solution(16263956002620162064)
XLA Ops:
  0.0 27.9 %shard_map.37 = bf16[10,64,2,768]{3,2,1,0:T(2,128)(2,1)S(1)} custom-call(s32[8]{0:T(128)} %pairs_ref.1, f32[10,128]{1,0:T(8,128)} %bitcast.3, bf16[8,1296,768]{2,1,0:T(8,128)(2,1)} %bitcast.2), custom_call_target="tpu_custom_call" | custom-call | flops 2600000000 | bytes 20000000 | tf_op jit(solution)/shard_map/pallas_call | solution.py:218
  27.9 1.3 %copy.5 = bf16[10,64,2,768]{3,2,1,0:T(2,128)(2,1)} copy(bf16[10,64,2,768]{3,2,1,0:T(2,128)(2,1)S(1)} %shard_map.37) | data formatting | bytes 3932160

commit v5 on v4

--- a/solution.py
+++ b/solution.py
@@ -17,7 +17,7 @@
 SETS = 8
 MESH = pl.DeviceIdType.MESH
 ORDER = [(dx, dy) for dx in (2, 1, 3, 0) for dy in (1, 0)]
-CUTS = 2
+CUTS = 4
 F32, BF16 = jnp.float32, jnp.bfloat16
 
 

time: 29.2 us -> 34.3 us (1.17)
  Pallas kernels: 27.9 us -> 33 us
    pallas_call x1, Pallas kernels: 27.9 us -> 33 us  [local(): pl.pallas_call(kernel, out_shape=jax.ShapeDtypeStruct((ROWS, 64, 2, COLS)...]
where the time goes in v5:
time: 34.3 us
  Pallas kernels  33 us (96%)
  local copies, waits for them, and re-layouts  1.27 us (4%)
    pallas_call x1, Pallas kernels, local(): pl.pallas_call(kernel, out_shape=jax.ShapeDtypeStruct((ROWS, 64, 2, COLS)...  33 us
    unnamed x1, local copies, waits for them, and re-layouts  1.27 us

profile of v5, /device:TPU:1, one launch (start us, length us, event | category | flops | bytes accessed | tf_op | source)
XLA Modules:
  0.0 34.3 jit_solution(13346436044476725387)
XLA Ops:
  0.0 33.0 %shard_map.37 = bf16[10,64,2,768]{3,2,1,0:T(2,128)(2,1)S(1)} custom-call(s32[8]{0:T(128)} %pairs_ref.1, f32[10,128]{1,0:T(8,128)} %bitcast.3, bf16[8,1296,768]{2,1,0:T(8,128)(2,1)} %bitcast.2), custom_call_target="tpu_custom_call" | custom-call | flops 2600000000 | bytes 20000000 | tf_op jit(solution)/shard_map/pallas_call | solution.py:218
  33.0 1.3 %copy.5 = bf16[10,64,2,768]{3,2,1,0:T(2,128)(2,1)} copy(bf16[10,64,2,768]{3,2,1,0:T(2,128)(2,1)S(1)} %shard_map.37) | data formatting | bytes 3932160

commit v6 on v4

--- a/solution.py
+++ b/solution.py
@@ -16,7 +16,7 @@
 SEG = 81
 SETS = 8
 MESH = pl.DeviceIdType.MESH
-ORDER = [(dx, dy) for dx in (2, 1, 3, 0) for dy in (1, 0)]
+ORDER = [(dx, dy) for dx in (1, 3, 2, 0) for dy in (1, 0)]
 CUTS = 2
 F32, BF16 = jnp.float32, jnp.bfloat16
 

time: 29.2 us -> 29.4 us (level)
  no operation moved by 1% of the time
where the time goes in v6:
time: 29.4 us; the launch traced here: 29.3 us
  Pallas kernels  28.1 us (96%)
  local copies, waits for them, and re-layouts  1.27 us (4%)
    pallas_call x1, Pallas kernels, local(): pl.pallas_call(kernel, out_shape=jax.ShapeDtypeStruct((ROWS, 64, 2, COLS)...  28.1 us
    unnamed x1, local copies, waits for them, and re-layouts  1.27 us

profile of v6, /device:TPU:1, one launch (start us, length us, event | category | flops | bytes accessed | tf_op | source)
XLA Modules:
  0.0 29.3 jit_solution(8442728582701971136)
XLA Ops:
  0.0 28.1 %shard_map.37 = bf16[10,64,2,768]{3,2,1,0:T(2,128)(2,1)S(1)} custom-call(s32[8]{0:T(128)} %pairs_ref.1, f32[10,128]{1,0:T(8,128)} %bitcast.3, bf16[8,1296,768]{2,1,0:T(8,128)(2,1)} %bitcast.2), custom_call_target="tpu_custom_call" | custom-call | flops 2600000000 | bytes 20000000 | tf_op jit(solution)/shard_map/pallas_call | solution.py:218
  28.1 1.3 %copy.5 = bf16[10,64,2,768]{3,2,1,0:T(2,128)(2,1)} copy(bf16[10,64,2,768]{3,2,1,0:T(2,128)(2,1)S(1)} %shard_map.37) | data formatting | bytes 3932160
